TPU v7x, 512 devices: a whole 4x4x16 slice. The times are simulated.
512 devices in a mesh: gx: 32 (over x, y, core), gy: 16 (over z).
Axes of the slice: x: 4, y: 4, z: 16, core: 2. Of those that a mesh axis runs over, the one named last changes fastest.
Arguments:
- right_side: float32 [2, 512, 2048], P(None, 'gx', 'gy'), may hold values from -160 to 160
- conductivity: float32 [512, 2048], P('gx', 'gy'), may hold values from 0.2 to 5
- leaf_inverse: float32 [128, 64, 128, 128], P('gx', 'gy'), may hold values from -1 to 4, as said below
- front_basis: float32 [512, 2048, 128], P('gx', 'gy'), may hold values from -0.25 to 0.25
- leaf_transfer: float32 [32, 16, 128, 128], P('gx', 'gy'), may hold values from -0.4375 to 0.4375
- node_transfer: float32 [32, 16, 8, 128, 128], P('gx', 'gy'), may hold values from -1 to 1, as said below
- leaf_front: float32 [32, 16, 128, 128], P('gx', 'gy'), may hold values from -1 to 1, as said below
- node_front: float32 [32, 16, 9, 128, 128], P('gx', 'gy'), may hold values from -1 to 1, as said below
Outputs:
- solution: float32 [2, 512, 2048], P(None, 'gx', 'gy')
- residual: float32 [2, 512, 2048], P(None, 'gx', 'gy')
- direction: float32 [2, 512, 2048], P(None, 'gx', 'gy')
Inputs may be any that keep to these rules, and one draw needn't show every extreme that they name: `leaf_inverse`: every block is symmetric and positive definite. `leaf_front`: every matrix is symmetric and positive definite. `node_front`: every matrix is symmetric and positive definite; entry h - 1 is the same for all tiles covered by one node of level h. `node_transfer`: entry h - 1 is the same for all tiles covered by one node of level h.
All inputs are finite; a program needn't handle non-finite values.
Results may differ from a plain program's by a relative error of at most 0.0001.
Values sent between devices are 32-bit elements; how exact they have to be, the bound alone decides.
A program may use at most 64 MiB of HBM per device.

v0:
```python
from functools import partial
import jax
import jax.numpy as jnp
from jax import lax
from jax.sharding import PartitionSpec as P

LBX = 4
LBY = 32
HIGHEST = lax.Precision.HIGHEST


def extended(cells, sides, width):
    for axis, dim in sides:
        count = lax.axis_size(axis)
        ends = count - 1
        head = lax.slice_in_dim(cells, 0, width, axis=dim)
        tail = lax.slice_in_dim(cells, cells.shape[dim] - width, cells.shape[dim], axis=dim)
        cells = jnp.concatenate(
            [
                lax.ppermute(tail, axis, [(i, (i + 1) % count) for i in range(ends)]),
                cells,
                lax.ppermute(head, axis, [((i + 1) % count, i) for i in range(ends)]),
            ],
            axis=dim,
        )
    return cells


def from_partner(value, axis, distance):
    mask = 2**distance
    pairs = [(source, source ^ mask) for source in range(lax.axis_size(axis))]
    return lax.ppermute(value, axis, pairs)


def operate_padded(padded, padded_k):
    extent_x = padded.shape[1] - 2
    extent_y = padded.shape[2] - 2
    center = padded[:, 1:-1, 1:-1]
    center_k = padded_k[1:-1, 1:-1]
    summed = jnp.zeros_like(center)
    for offset_x, offset_y in ((2, 1), (0, 1), (1, 2), (1, 0)):
        beside = padded[:, offset_x : offset_x + extent_x, offset_y : offset_y + extent_y]
        beside_k = padded_k[offset_x : offset_x + extent_x, offset_y : offset_y + extent_y]
        summed = summed + 0.5 * (center_k + beside_k) * (center - beside)
    return summed


def stencil(values, conductivity):
    stacked = jnp.concatenate([values, conductivity[None]], axis=0)
    padded = extended(stacked, (("gx", 1), ("gy", 2)), 1)
    return operate_padded(padded[:-1], padded[-1])


def leaf_apply(values, leaf_inverse):
    count_s, extent_x, extent_y = values.shape
    blocks_x = extent_x // LBX
    blocks_y = extent_y // LBY
    grouped = values.reshape(count_s, blocks_x, LBX, blocks_y, LBY).transpose(0, 1, 3, 2, 4)
    grouped = grouped.reshape(count_s, blocks_x, blocks_y, LBX * LBY)
    mapped = jnp.einsum("xyij,sxyj->sxyi", leaf_inverse, grouped, precision=HIGHEST)
    mapped = mapped.reshape(count_s, blocks_x, blocks_y, LBX, LBY).transpose(0, 1, 3, 2, 4)
    return mapped.reshape(count_s, extent_x, extent_y)


def spread_tree(coeffs, leaf_transfer, node_transfer, leaf_front, node_front):
    levels = lax.axis_size(("gx", "gy")).bit_length() - 1
    leaf_t = leaf_transfer[0, 0]
    leaf_f = leaf_front[0, 0]
    node_t = node_transfer[0, 0]
    node_f = node_front[0, 0]
    uppers = [coeffs]
    moving = jnp.dot(coeffs, leaf_t, precision=HIGHEST)
    for height in range(1, levels + 1):
        partner = from_partner(moving, ("gx", "gy"), height - 1)
        summed = moving + partner
        uppers.append(summed)
        if height < levels:
            moving = jnp.dot(summed, node_t[height - 1], precision=HIGHEST)
    downward = jnp.dot(uppers[levels], node_f[levels - 1], precision=HIGHEST)
    for height in range(levels, 1, -1):
        downward = jnp.dot(downward, node_t[height - 2].T, precision=HIGHEST) + jnp.dot(
            uppers[height - 1], node_f[height - 2], precision=HIGHEST
        )
    return jnp.dot(downward, leaf_t.T, precision=HIGHEST) + jnp.dot(
        coeffs, leaf_f, precision=HIGHEST
    )


def precondition(
    values, leaf_inverse, front_basis, leaf_transfer, node_transfer, leaf_front, node_front
):
    near = leaf_apply(values, leaf_inverse)
    coeffs = jnp.einsum("sab,abk->sk", values, front_basis, precision=HIGHEST)
    spread = spread_tree(coeffs, leaf_transfer, node_transfer, leaf_front, node_front)
    return near + jnp.einsum("sk,abk->sab", spread, front_basis, precision=HIGHEST)


def on_device(
    right_side,
    conductivity,
    leaf_inverse,
    front_basis,
    leaf_transfer,
    node_transfer,
    leaf_front,
    node_front,
):
    apply_inverse = partial(
        precondition,
        leaf_inverse=leaf_inverse,
        front_basis=front_basis,
        leaf_transfer=leaf_transfer,
        node_transfer=node_transfer,
        leaf_front=leaf_front,
        node_front=node_front,
    )
    first_z = apply_inverse(right_side)
    local_rz = jnp.sum(right_side * first_z, axis=(1, 2))
    rz_old = lax.psum(local_rz, ("gx", "gy"))
    applied = stencil(first_z, conductivity)
    curvature = lax.psum(jnp.sum(first_z * applied, axis=(1, 2)), ("gx", "gy"))
    step_size = (rz_old / curvature)[:, None, None]
    solution = step_size * first_z
    residual = right_side - step_size * applied
    second_z = apply_inverse(residual)
    rz_new = lax.psum(jnp.sum(residual * second_z, axis=(1, 2)), ("gx", "gy"))
    direction = second_z + (rz_new / rz_old)[:, None, None] * first_z
    return (solution, residual, direction)


def solution(mesh):
    return jax.shard_map(
        on_device,
        mesh=mesh,
        in_specs=(
            P(None, "gx", "gy"),
            P("gx", "gy"),
            P("gx", "gy", None, None),
            P("gx", "gy", None),
            P("gx", "gy", None, None),
            P("gx", "gy", None, None, None),
            P("gx", "gy", None, None),
            P("gx", "gy", None, None, None),
        ),
        out_specs=(P(None, "gx", "gy"), P(None, "gx", "gy"), P(None, "gx", "gy")),
        check_vma=False,
    )
```

profile of v0, /device:TPU:1, one launch (start us, length us, event | category | flops | bytes accessed | tf_op | source)
XLA Modules:
  0.0 377.9 jit_solution(12129984315452648051)
XLA Ops:
  0.7 1.2 copy-done
  1.9 1.3 convolution_bitcast_fusion.3
  3.4 4.4 %collective-permute-start = (f32[2,128]{1,0:T(2,128)S(1)}, f32[2,128]{1,0:T(2,128)S(1)}, u32[]{:S(2)}, u32[]{:S(2)}) collective-permute-start(f32[2,128]{1,0:T(2,128)S(1)} %fusion.94), channel_id=1, source_target_pairs={{0,1},{1,0},{2,3},{3,2},{4,5},{5,4},{6,7},{7,6},{8,9},{9,8},{10,11... | collective-permute-start | bytes 3080 | tf_op jit(solution)/shard_map/ppermute | solution.py:32
  7.7 0.9 collective-permute-done
  8.8 4.9 %collective-permute-start.1 = (f32[2,128]{1,0:T(2,128)S(1)}, f32[2,128]{1,0:T(2,128)S(1)}, u32[]{:S(2)}, u32[]{:S(2)}) collective-permute-start(f32[2,128]{1,0:T(2,128)S(1)} %fusion.86), channel_id=1, source_target_pairs={{0,2},{1,3},{2,0},{3,1},{4,6},{5,7},{6,4},{7,5},{8,10},{9,11},{10,... | collective-permute-start | bytes 3080 | tf_op jit(solution)/shard_map/ppermute | solution.py:32
  13.8 0.9 collective-permute-done.1
  14.9 8.8 %collective-permute-start.2 = (f32[2,128]{1,0:T(2,128)S(1)}, f32[2,128]{1,0:T(2,128)S(1)}, u32[]{:S(2)}, u32[]{:S(2)}) collective-permute-start(f32[2,128]{1,0:T(2,128)S(1)} %fusion.78), channel_id=1, source_target_pairs={{0,4},{1,5},{2,6},{3,7},{4,0},{5,1},{6,2},{7,3},{8,12},{9,13},{10,... | collective-permute-start | bytes 3080 | tf_op jit(solution)/shard_map/ppermute | solution.py:32
  23.7 0.9 collective-permute-done.2
  24.8 13.1 %collective-permute-start.3 = (f32[2,128]{1,0:T(2,128)S(1)}, f32[2,128]{1,0:T(2,128)S(1)}, u32[]{:S(2)}, u32[]{:S(2)}) collective-permute-start(f32[2,128]{1,0:T(2,128)S(1)} %fusion.70), channel_id=1, source_target_pairs={{0,8},{1,9},{2,10},{3,11},{4,12},{5,13},{6,14},{7,15},{8,0},{9,1},... | collective-permute-start | bytes 3080 | tf_op jit(solution)/shard_map/ppermute | solution.py:32
  37.9 0.9 collective-permute-done.3
  39.0 9.2 %collective-permute-start.4 = (f32[2,128]{1,0:T(2,128)S(1)}, f32[2,128]{1,0:T(2,128)S(1)}, u32[]{:S(2)}, u32[]{:S(2)}) collective-permute-start(f32[2,128]{1,0:T(2,128)S(1)} %fusion.62), channel_id=1, source_target_pairs={{0,16},{1,17},{2,18},{3,19},{4,20},{5,21},{6,22},{7,23},{8,24},{9,... | collective-permute-start | bytes 3080 | tf_op jit(solution)/shard_map/ppermute | solution.py:32
  49.1 1.9 collective-permute-start.5
  51.1 2.4 collective-permute-done.5
  53.6 2.5 collective-permute-start.6
  56.2 3.3 collective-permute-done.6
  59.6 1.9 collective-permute-start.7
  62.5 1.4 collective-permute-done.7
  64.1 2.5 collective-permute-start.8
  66.6 1.7 convolution_bitcast_fusion.1
  68.6 1.4 collective-permute-done.8
  74.2 1.0 convolution_add_fusion.1
  75.2 6.8 %collective-permute-start.10 = (f32[3,1,128]{2,0,1:T(4,128)S(1)}, f32[3,1,128]{2,0,1:T(4,128)S(1)}, u32[]{:S(2)}, u32[]{:S(2)}) collective-permute-start(f32[3,1,128]{2,0,1:T(4,128)S(1)} %get-tuple-element.18), channel_id=1, source_target_pairs={{16,0},{32,16},{48,32},{64,48},{80,64},{96,80},{112,96},{128,112},... | collective-permute-start | bytes 4616 | tf_op jit(solution)/shard_map/ppermute | solution.py:22
  82.0 1.9 collective-permute-start.9
  83.9 1.1 collective-permute-done.9
  85.2 1.6 collective-permute-start.11
  86.8 1.3 collective-permute-start.12
  88.1 3.4 collective-permute-done.12
  92.7 109.6 %all-reduce = (f32[2]{0:T(128)S(1)}, f32[2]{0:T(128)S(1)}) all-reduce(f32[2]{0:T(128)S(1)} %get-tuple-element.7, f32[2]{0:T(128)S(1)} %get-tuple-element.6), channel_id=1, replica_groups=mesh['gx'=32,'gy'=16] {'gx','gy'}, use_global_device_ids=true, to_apply=%region_1.0 | all-reduce | flops 4 | bytes 32 | tf_op jit(solution)/shard_map/psum | solution.py:119
  204.2 1.9 collective-permute-start.13
  206.2 2.4 collective-permute-done.13
  208.7 1.9 collective-permute-start.14
  210.6 3.3 collective-permute-done.14
  214.1 4.0 %collective-permute-start.15 = (f32[2,128]{1,0:T(2,128)S(1)}, f32[2,128]{1,0:T(2,128)S(1)}, u32[]{:S(2)}, u32[]{:S(2)}) collective-permute-start(f32[2,128]{1,0:T(2,128)S(1)} %fusion.74), channel_id=1, source_target_pairs={{0,4},{1,5},{2,6},{3,7},{4,0},{5,1},{6,2},{7,3},{8,12},{9,13},{10,... | collective-permute-start | bytes 3080 | tf_op jit(solution)/shard_map/ppermute | solution.py:32
  218.1 4.2 %collective-permute-done.15 = f32[2,128]{1,0:T(2,128)S(1)} collective-permute-done((f32[2,128]{1,0:T(2,128)S(1)}, f32[2,128]{1,0:T(2,128)S(1)}, u32[]{:S(2)}, u32[]{:S(2)}) %collective-permute-start.15) | collective-permute-done | bytes 1056 | tf_op jit(solution)/shard_map/ppermute | solution.py:32
  222.5 8.2 %collective-permute-start.16 = (f32[2,128]{1,0:T(2,128)S(1)}, f32[2,128]{1,0:T(2,128)S(1)}, u32[]{:S(2)}, u32[]{:S(2)}) collective-permute-start(f32[2,128]{1,0:T(2,128)S(1)} %fusion.66), channel_id=1, source_target_pairs={{0,8},{1,9},{2,10},{3,11},{4,12},{5,13},{6,14},{7,15},{8,0},{9,1},... | collective-permute-start | bytes 3080 | tf_op jit(solution)/shard_map/ppermute | solution.py:32
  230.7 4.8 %collective-permute-done.16 = f32[2,128]{1,0:T(2,128)S(1)} collective-permute-done((f32[2,128]{1,0:T(2,128)S(1)}, f32[2,128]{1,0:T(2,128)S(1)}, u32[]{:S(2)}, u32[]{:S(2)}) %collective-permute-start.16) | collective-permute-done | bytes 1056 | tf_op jit(solution)/shard_map/ppermute | solution.py:32
  236.0 7.7 %collective-permute-start.17 = (f32[2,128]{1,0:T(2,128)S(1)}, f32[2,128]{1,0:T(2,128)S(1)}, u32[]{:S(2)}, u32[]{:S(2)}) collective-permute-start(f32[2,128]{1,0:T(2,128)S(1)} %fusion.58), channel_id=1, source_target_pairs={{0,16},{1,17},{2,18},{3,19},{4,20},{5,21},{6,22},{7,23},{8,24},{9,... | collective-permute-start | bytes 3080 | tf_op jit(solution)/shard_map/ppermute | solution.py:32
  245.1 1.9 collective-permute-start.18
  247.0 2.4 collective-permute-done.18
  250.0 2.5 collective-permute-start.19
  252.5 3.3 collective-permute-done.19
  256.3 1.9 collective-permute-start.20
  258.5 2.2 collective-permute-done.20
  261.6 2.8 collective-permute-start.21
  264.3 1.7 convolution_bitcast_fusion
  267.7 0.9 convolution_add_fusion.10
  273.5 1.1 multiply_reduce_fusion
  274.6 101.4 %psum.23 = f32[2]{0:T(128)S(1)} all-reduce(f32[2]{0:T(128)S(1)} %get-tuple-element.21), channel_id=1, replica_groups=mesh['gx'=32,'gy'=16] {'gx','gy'}, use_global_device_ids=true, to_apply=%region_5.0 | all-reduce | flops 2 | bytes 16 | tf_op jit(solution)/shard_map/psum | solution.py:126
  (126 shorter events, 23.7 us)
Async XLA Ops:
  0.6 1.2 copy-start
  0.6 2.5 copy-start.4
  0.7 8.0 %copy-start.1 = (f32[1,1,8,128,128]{4,3,2,1,0:T(8,128)S(1)}, f32[1,1,8,128,128]{4,3,2,1,0:T(8,128)}, u32[]{:S(2)}) copy-start(f32[1,1,8,128,128]{4,3,2,1,0:T(8,128)} %param.13) | copy-start | bytes 1572868
  0.7 65.9 %copy-start.2 = (f32[4,4,128,128]{3,2,1,0:T(8,128)S(1)}, f32[4,4,128,128]{3,2,1,0:T(8,128)}, u32[]{:S(2)}) copy-start(f32[4,4,128,128]{3,2,1,0:T(8,128)} %param.10) | copy-start | bytes 3145732
  3.4 5.3 %collective-permute-start = (f32[2,128]{1,0:T(2,128)S(1)}, f32[2,128]{1,0:T(2,128)S(1)}, u32[]{:S(2)}, u32[]{:S(2)}) collective-permute-start(f32[2,128]{1,0:T(2,128)S(1)} %fusion.94), channel_id=1, source_target_pairs={{0,1},{1,0},{2,3},{3,2},{4,5},{5,4},{6,7},{7,6},{8,9},{9,8},{10,11... | collective-permute-start | bytes 3080 | tf_op jit(solution)/shard_map/ppermute | solution.py:32
  8.8 5.9 %collective-permute-start.1 = (f32[2,128]{1,0:T(2,128)S(1)}, f32[2,128]{1,0:T(2,128)S(1)}, u32[]{:S(2)}, u32[]{:S(2)}) collective-permute-start(f32[2,128]{1,0:T(2,128)S(1)} %fusion.86), channel_id=1, source_target_pairs={{0,2},{1,3},{2,0},{3,1},{4,6},{5,7},{6,4},{7,5},{8,10},{9,11},{10,... | collective-permute-start | bytes 3080 | tf_op jit(solution)/shard_map/ppermute | solution.py:32
  14.9 9.8 %collective-permute-start.2 = (f32[2,128]{1,0:T(2,128)S(1)}, f32[2,128]{1,0:T(2,128)S(1)}, u32[]{:S(2)}, u32[]{:S(2)}) collective-permute-start(f32[2,128]{1,0:T(2,128)S(1)} %fusion.78), channel_id=1, source_target_pairs={{0,4},{1,5},{2,6},{3,7},{4,0},{5,1},{6,2},{7,3},{8,12},{9,13},{10,... | collective-permute-start | bytes 3080 | tf_op jit(solution)/shard_map/ppermute | solution.py:32
  24.8 14.0 %collective-permute-start.3 = (f32[2,128]{1,0:T(2,128)S(1)}, f32[2,128]{1,0:T(2,128)S(1)}, u32[]{:S(2)}, u32[]{:S(2)}) collective-permute-start(f32[2,128]{1,0:T(2,128)S(1)} %fusion.70), channel_id=1, source_target_pairs={{0,8},{1,9},{2,10},{3,11},{4,12},{5,13},{6,14},{7,15},{8,0},{9,1},... | collective-permute-start | bytes 3080 | tf_op jit(solution)/shard_map/ppermute | solution.py:32
  39.0 10.0 %collective-permute-start.4 = (f32[2,128]{1,0:T(2,128)S(1)}, f32[2,128]{1,0:T(2,128)S(1)}, u32[]{:S(2)}, u32[]{:S(2)}) collective-permute-start(f32[2,128]{1,0:T(2,128)S(1)} %fusion.62), channel_id=1, source_target_pairs={{0,16},{1,17},{2,18},{3,19},{4,20},{5,21},{6,22},{7,23},{8,24},{9,... | collective-permute-start | bytes 3080 | tf_op jit(solution)/shard_map/ppermute | solution.py:32
  49.1 4.3 %collective-permute-start.5 = (f32[2,128]{1,0:T(2,128)S(1)}, f32[2,128]{1,0:T(2,128)S(1)}, u32[]{:S(2)}, u32[]{:S(2)}) collective-permute-start(f32[2,128]{1,0:T(2,128)S(1)} %fusion.54), channel_id=1, source_target_pairs={{0,32},{1,33},{2,34},{3,35},{4,36},{5,37},{6,38},{7,39},{8,40},{9,... | collective-permute-start | bytes 3080 | tf_op jit(solution)/shard_map/ppermute | solution.py:32
  53.6 5.8 %collective-permute-start.6 = (f32[2,128]{1,0:T(2,128)S(1)}, f32[2,128]{1,0:T(2,128)S(1)}, u32[]{:S(2)}, u32[]{:S(2)}) collective-permute-start(f32[2,128]{1,0:T(2,128)S(1)} %fusion.46), channel_id=1, source_target_pairs={{0,64},{1,65},{2,66},{3,67},{4,68},{5,69},{6,70},{7,71},{8,72},{9,... | collective-permute-start | bytes 3080 | tf_op jit(solution)/shard_map/ppermute | solution.py:32
  59.6 4.3 %collective-permute-start.7 = (f32[2,128]{1,0:T(2,128)S(1)}, f32[2,128]{1,0:T(2,128)S(1)}, u32[]{:S(2)}, u32[]{:S(2)}) collective-permute-start(f32[2,128]{1,0:T(2,128)S(1)} %fusion.38), channel_id=1, source_target_pairs={{0,128},{1,129},{2,130},{3,131},{4,132},{5,133},{6,134},{7,135},{8... | collective-permute-start | bytes 3080 | tf_op jit(solution)/shard_map/ppermute | solution.py:32
  64.1 6.0 %copy-start.3 = (f32[1,1,9,128,128]{4,3,2,1,0:T(8,128)S(1)}, f32[1,1,9,128,128]{4,3,2,1,0:T(8,128)}, u32[]{:S(2)}) copy-start(f32[1,1,9,128,128]{4,3,2,1,0:T(8,128)} %param.15) | copy-start | bytes 1769476
  64.1 6.0 %collective-permute-start.8 = (f32[2,128]{1,0:T(2,128)S(1)}, f32[2,128]{1,0:T(2,128)S(1)}, u32[]{:S(2)}, u32[]{:S(2)}) collective-permute-start(f32[2,128]{1,0:T(2,128)S(1)} %fusion.30), channel_id=1, source_target_pairs={{0,256},{1,257},{2,258},{3,259},{4,260},{5,261},{6,262},{7,263},{8... | collective-permute-start | bytes 3080 | tf_op jit(solution)/shard_map/ppermute | solution.py:32
  73.1 0.9 copy-start.6
  74.2 1.0 copy-start.7
  75.2 8.8 %collective-permute-start.10 = (f32[3,1,128]{2,0,1:T(4,128)S(1)}, f32[3,1,128]{2,0,1:T(4,128)S(1)}, u32[]{:S(2)}, u32[]{:S(2)}) collective-permute-start(f32[3,1,128]{2,0,1:T(4,128)S(1)} %get-tuple-element.18), channel_id=1, source_target_pairs={{16,0},{32,16},{48,32},{64,48},{80,64},{96,80},{112,96},{128,112},... | collective-permute-start | bytes 4616 | tf_op jit(solution)/shard_map/ppermute | solution.py:22
  82.0 3.1 collective-permute-start.9
  85.2 3.0 collective-permute-start.11
  86.8 4.7 %collective-permute-start.12 = (f32[3,18,1]{2,0,1:T(4,128)S(1)}, f32[3,18,1]{2,0,1:T(4,128)S(1)}, u32[]{:S(2)}, u32[]{:S(2)}) collective-permute-start(f32[3,18,1]{2,0,1:T(4,128)S(1)} %get-tuple-element.11), channel_id=1, source_target_pairs={{1,0},{2,1},{3,2},{4,3},{5,4},{6,5},{7,6},{8,7},{9,8},{10,9},{11,1... | collective-permute-start | bytes 656 | tf_op jit(solution)/shard_map/ppermute | solution.py:22
  91.7 0.7 copy-start.5
  202.3 0.6 copy-start.18
  202.9 0.5 copy-start.16
  204.2 4.3 %collective-permute-start.13 = (f32[2,128]{1,0:T(2,128)S(1)}, f32[2,128]{1,0:T(2,128)S(1)}, u32[]{:S(2)}, u32[]{:S(2)}) collective-permute-start(f32[2,128]{1,0:T(2,128)S(1)} %fusion.90), channel_id=1, source_target_pairs={{0,1},{1,0},{2,3},{3,2},{4,5},{5,4},{6,7},{7,6},{8,9},{9,8},{10,11... | collective-permute-start | bytes 3080 | tf_op jit(solution)/shard_map/ppermute | solution.py:32
  208.7 5.2 %collective-permute-start.14 = (f32[2,128]{1,0:T(2,128)S(1)}, f32[2,128]{1,0:T(2,128)S(1)}, u32[]{:S(2)}, u32[]{:S(2)}) collective-permute-start(f32[2,128]{1,0:T(2,128)S(1)} %fusion.82), channel_id=1, source_target_pairs={{0,2},{1,3},{2,0},{3,1},{4,6},{5,7},{6,4},{7,5},{8,10},{9,11},{10,... | collective-permute-start | bytes 3080 | tf_op jit(solution)/shard_map/ppermute | solution.py:32
  214.1 8.2 %collective-permute-start.15 = (f32[2,128]{1,0:T(2,128)S(1)}, f32[2,128]{1,0:T(2,128)S(1)}, u32[]{:S(2)}, u32[]{:S(2)}) collective-permute-start(f32[2,128]{1,0:T(2,128)S(1)} %fusion.74), channel_id=1, source_target_pairs={{0,4},{1,5},{2,6},{3,7},{4,0},{5,1},{6,2},{7,3},{8,12},{9,13},{10,... | collective-permute-start | bytes 3080 | tf_op jit(solution)/shard_map/ppermute | solution.py:32
  222.5 13.0 %collective-permute-start.16 = (f32[2,128]{1,0:T(2,128)S(1)}, f32[2,128]{1,0:T(2,128)S(1)}, u32[]{:S(2)}, u32[]{:S(2)}) collective-permute-start(f32[2,128]{1,0:T(2,128)S(1)} %fusion.66), channel_id=1, source_target_pairs={{0,8},{1,9},{2,10},{3,11},{4,12},{5,13},{6,14},{7,15},{8,0},{9,1},... | collective-permute-start | bytes 3080 | tf_op jit(solution)/shard_map/ppermute | solution.py:32
  235.5 0.5 copy-start.8
  236.0 8.5 %collective-permute-start.17 = (f32[2,128]{1,0:T(2,128)S(1)}, f32[2,128]{1,0:T(2,128)S(1)}, u32[]{:S(2)}, u32[]{:S(2)}) collective-permute-start(f32[2,128]{1,0:T(2,128)S(1)} %fusion.58), channel_id=1, source_target_pairs={{0,16},{1,17},{2,18},{3,19},{4,20},{5,21},{6,22},{7,23},{8,24},{9,... | collective-permute-start | bytes 3080 | tf_op jit(solution)/shard_map/ppermute | solution.py:32
  244.5 0.6 copy-start.10
  245.1 4.3 %collective-permute-start.18 = (f32[2,128]{1,0:T(2,128)S(1)}, f32[2,128]{1,0:T(2,128)S(1)}, u32[]{:S(2)}, u32[]{:S(2)}) collective-permute-start(f32[2,128]{1,0:T(2,128)S(1)} %fusion.50), channel_id=1, source_target_pairs={{0,32},{1,33},{2,34},{3,35},{4,36},{5,37},{6,38},{7,39},{8,40},{9,... | collective-permute-start | bytes 3080 | tf_op jit(solution)/shard_map/ppermute | solution.py:32
  249.4 0.6 copy-start.12
  250.0 5.8 %collective-permute-start.19 = (f32[2,128]{1,0:T(2,128)S(1)}, f32[2,128]{1,0:T(2,128)S(1)}, u32[]{:S(2)}, u32[]{:S(2)}) collective-permute-start(f32[2,128]{1,0:T(2,128)S(1)} %fusion.42), channel_id=1, source_target_pairs={{0,64},{1,65},{2,66},{3,67},{4,68},{5,69},{6,70},{7,71},{8,72},{9,... | collective-permute-start | bytes 3080 | tf_op jit(solution)/shard_map/ppermute | solution.py:32
  255.8 0.6 copy-start.14
  256.3 4.4 %collective-permute-start.20 = (f32[2,128]{1,0:T(2,128)S(1)}, f32[2,128]{1,0:T(2,128)}, u32[]{:S(2)}, u32[]{:S(2)}) collective-permute-start(f32[2,128]{1,0:T(2,128)S(1)} %fusion.34), channel_id=1, source_target_pairs={{0,128},{1,129},{2,130},{3,131},{4,132},{5,133},{6,134},{7,135},{8... | collective-permute-start | bytes 3080 | tf_op jit(solution)/shard_map/ppermute | solution.py:32
  261.6 5.8 %collective-permute-start.21 = (f32[2,128]{1,0:T(2,128)S(1)}, f32[2,128]{1,0:T(2,128)S(1)}, u32[]{:S(2)}, u32[]{:S(2)}) collective-permute-start(f32[2,128]{1,0:T(2,128)S(1)} %fusion.26), channel_id=1, source_target_pairs={{0,256},{1,257},{2,258},{3,259},{4,260},{5,261},{6,262},{7,263},{8... | collective-permute-start | bytes 3080 | tf_op jit(solution)/shard_map/ppermute | solution.py:32
  268.6 0.7 copy-start.15
  269.4 0.7 copy-start.13
  270.3 0.7 copy-start.11
  271.1 0.7 copy-start.9
  274.6 101.4 %copy-start.19 = (f32[2]{0:T(128)S(1)}, f32[2]{0:T(128)}, u32[]{:S(2)}) copy-start(f32[2]{0:T(128)} %copy-done.18) | copy-start | bytes 28
  376.0 0.6 copy-start.17
where the time goes:
time: 379 us; the launch traced here: 378 us
  blocking collectives  211 us (56%)
  starting transfers between devices  93.8 us (25%)
  waiting for transfers between devices  41.5 us (11%)
  matrix products  18.7 us (5%)
  local copies, waits for them, and re-layouts  11.2 us (3%)
    psum x1, blocking collectives, on_device(): rz_old = lax.psum(local_rz, ('gx', 'gy'))  110 us
    psum x1, blocking collectives, on_device(): rz_new = lax.psum(jnp.sum(residual * second_z, axis=(1, 2)), ('gx', 'gy'))  101 us
    ppermute x18, starting transfers between devices, from_partner(): return lax.ppermute(value, axis, pairs)  82.1 us
    ppermute x18, waiting for transfers between devices, from_partner(): return lax.ppermute(value, axis, pairs)  37 us
    unnamed x44, local copies, waits for them, and re-layouts  9.48 us
    ppermute x2, starting transfers between devices, extended(): lax.ppermute(head, axis, [((i + 1) % count, i) for i in range(ends)])  8.12 us
  transfers between devices with their start and end apart: 22, of which 20 were waited for; matrix products, arithmetic and copies ran while one was open for 2% of the time, Pallas kernels for 0%

commit v1 on v0

--- a/solution.py
+++ b/solution.py
@@ -116,7 +116,8 @@
     )
     first_z = apply_inverse(right_side)
     local_rz = jnp.sum(right_side * first_z, axis=(1, 2))
-    rz_old = lax.psum(local_rz, ("gx", "gy"))
+    partial_2 = lax.psum(local_rz, "gy")
+    rz_old = lax.psum(partial_2, "gx")
     applied = stencil(first_z, conductivity)
     curvature = lax.psum(jnp.sum(first_z * applied, axis=(1, 2)), ("gx", "gy"))
     step_size = (rz_old / curvature)[:, None, None]

time: 379 us -> 468 us (1.23)
  blocking collectives: 211 us -> 300 us
  waiting for transfers between devices: 41.5 us -> 36.3 us
  starting transfers between devices: 93.8 us -> 98.8 us
    psum x1 -> x3, blocking collectives: 110 us -> 196 us  [the longest x1 98.8 us: on_device(): curvature = lax.psum(jnp.sum(first_z * applied, axis=(1, 2)), ('gx', 'gy'))]
    ppermute x18, waiting for transfers between devices: 37 us -> 31.8 us  [from_partner(): return lax.ppermute(value, axis, pairs)]
    ppermute x18, starting transfers between devices: 82.1 us -> 87.1 us  [from_partner(): return lax.ppermute(value, axis, pairs)]
  transfers between devices with their start and end apart: 22 -> 22, of which waited for: 20 -> 20; matrix products, arithmetic and copies ran while one was open for 2% -> 1% of each run, Pallas kernels for 0% -> 0%
where the time goes in v1:
time: 468 us; the launch traced here: 467 us
  blocking collectives  300 us (64%)
  starting transfers between devices  98.8 us (21%)
  waiting for transfers between devices  36.3 us (8%)
  matrix products  18.6 us (4%)
  local copies, waits for them, and re-layouts  10.9 us (2%)
    psum x1, blocking collectives, on_device(): rz_new = lax.psum(jnp.sum(residual * second_z, axis=(1, 2)), ('gx', 'gy'))  104 us
    psum x1, blocking collectives, on_device(): curvature = lax.psum(jnp.sum(first_z * applied, axis=(1, 2)), ('gx', 'gy'))  98.8 us
    ppermute x18, starting transfers between devices, from_partner(): return lax.ppermute(value, axis, pairs)  87.1 us
    psum x1, blocking collectives, on_device(): rz_old = lax.psum(partial_2, 'gx')  71.3 us
    ppermute x18, waiting for transfers between devices, from_partner(): return lax.ppermute(value, axis, pairs)  31.8 us
    psum x1, blocking collectives, on_device(): partial_2 = lax.psum(local_rz, 'gy')  26.3 us
  transfers between devices with their start and end apart: 22, of which 20 were waited for; matrix products, arithmetic and copies ran while one was open for 1% of the time, Pallas kernels for 0%

profile of v1, /device:TPU:1, one launch (start us, length us, event | category | flops | bytes accessed | tf_op | source)
XLA Modules:
  0.0 466.7 jit_solution(892643002577639793)
XLA Ops:
  0.7 1.2 copy-done
  1.9 1.3 convolution_bitcast_fusion.3
  3.4 4.4 collective-permute-start
  7.7 0.9 collective-permute-done
  8.8 4.9 %collective-permute-start.1 = (f32[2,128]{1,0:T(2,128)S(1)}, f32[2,128]{1,0:T(2,128)S(1)}, u32[]{:S(2)}, u32[]{:S(2)}) collective-permute-start(f32[2,128]{1,0:T(2,128)S(1)} %fusion.86), channel_id=1, source_target_pairs={{0,2},{1,3},{2,0},{3,1},{4,6},{5,7},{6,4},{7,5},{8,10},{9,11},{10,... | collective-permute-start | bytes 3080 | tf_op jit(solution)/shard_map/ppermute | solution.py:32
  13.8 0.9 collective-permute-done.1
  14.9 8.8 %collective-permute-start.2 = (f32[2,128]{1,0:T(2,128)S(1)}, f32[2,128]{1,0:T(2,128)S(1)}, u32[]{:S(2)}, u32[]{:S(2)}) collective-permute-start(f32[2,128]{1,0:T(2,128)S(1)} %fusion.78), channel_id=1, source_target_pairs={{0,4},{1,5},{2,6},{3,7},{4,0},{5,1},{6,2},{7,3},{8,12},{9,13},{10,... | collective-permute-start | bytes 3080 | tf_op jit(solution)/shard_map/ppermute | solution.py:32
  23.7 0.9 collective-permute-done.2
  24.8 13.1 %collective-permute-start.3 = (f32[2,128]{1,0:T(2,128)S(1)}, f32[2,128]{1,0:T(2,128)S(1)}, u32[]{:S(2)}, u32[]{:S(2)}) collective-permute-start(f32[2,128]{1,0:T(2,128)S(1)} %fusion.70), channel_id=1, source_target_pairs={{0,8},{1,9},{2,10},{3,11},{4,12},{5,13},{6,14},{7,15},{8,0},{9,1},... | collective-permute-start | bytes 3080 | tf_op jit(solution)/shard_map/ppermute | solution.py:32
  37.9 0.9 collective-permute-done.3
  39.0 9.2 %collective-permute-start.4 = (f32[2,128]{1,0:T(2,128)S(1)}, f32[2,128]{1,0:T(2,128)S(1)}, u32[]{:S(2)}, u32[]{:S(2)}) collective-permute-start(f32[2,128]{1,0:T(2,128)S(1)} %fusion.62), channel_id=1, source_target_pairs={{0,16},{1,17},{2,18},{3,19},{4,20},{5,21},{6,22},{7,23},{8,24},{9,... | collective-permute-start | bytes 3080 | tf_op jit(solution)/shard_map/ppermute | solution.py:32
  49.1 1.9 collective-permute-start.5
  51.1 2.4 collective-permute-done.5
  53.6 2.5 collective-permute-start.6
  56.2 3.3 collective-permute-done.6
  59.6 1.9 collective-permute-start.7
  62.5 1.4 collective-permute-done.7
  64.1 2.5 collective-permute-start.8
  66.6 1.7 convolution_bitcast_fusion.1
  68.6 1.4 collective-permute-done.8
  74.2 1.0 convolution_add_fusion.1
  75.2 6.8 %collective-permute-start.10 = (f32[3,1,128]{2,0,1:T(4,128)S(1)}, f32[3,1,128]{2,0,1:T(4,128)S(1)}, u32[]{:S(2)}, u32[]{:S(2)}) collective-permute-start(f32[3,1,128]{2,0,1:T(4,128)S(1)} %get-tuple-element.16), channel_id=1, source_target_pairs={{16,0},{32,16},{48,32},{64,48},{80,64},{96,80},{112,96},{128,112},... | collective-permute-start | bytes 4616 | tf_op jit(solution)/shard_map/ppermute | solution.py:22
  82.0 1.9 collective-permute-start.9
  83.9 1.1 collective-permute-done.9
  85.2 1.6 collective-permute-start.11
  86.8 1.3 collective-permute-start.12
  88.1 3.4 collective-permute-done.12
  92.7 26.3 %psum.28 = f32[2]{0:T(128)S(1)} all-reduce(f32[2]{0:T(128)S(1)} %get-tuple-element.7), channel_id=1, replica_groups=mesh['gx'=32,'gy'=16] {'gy'}, use_global_device_ids=true, to_apply=%region_1.0 | all-reduce | flops 2 | bytes 16 | tf_op jit(solution)/shard_map/psum | solution.py:119
  119.0 71.3 %psum.29 = f32[2]{0:T(128)S(1)} all-reduce(f32[2]{0:T(128)S(1)} %psum.28), channel_id=1, replica_groups=mesh['gx'=32,'gy'=16] {'gx'}, use_global_device_ids=true, to_apply=%region_2.0 | all-reduce | flops 2 | bytes 16 | tf_op jit(solution)/shard_map/psum | solution.py:120
  190.4 98.8 %psum.30 = f32[2]{0:T(128)S(1)} all-reduce(f32[2]{0:T(128)S(1)} %get-tuple-element.6), channel_id=1, replica_groups=mesh['gx'=32,'gy'=16] {'gx','gy'}, use_global_device_ids=true, to_apply=%region_4.0 | all-reduce | flops 2 | bytes 16 | tf_op jit(solution)/shard_map/psum | solution.py:122
  290.6 3.7 collective-permute-start.13
  295.4 3.0 collective-permute-start.14
  298.4 2.2 collective-permute-done.14
  300.8 5.1 %collective-permute-start.15 = (f32[2,128]{1,0:T(2,128)S(1)}, f32[2,128]{1,0:T(2,128)S(1)}, u32[]{:S(2)}, u32[]{:S(2)}) collective-permute-start(f32[2,128]{1,0:T(2,128)S(1)} %fusion.74), channel_id=1, source_target_pairs={{0,4},{1,5},{2,6},{3,7},{4,0},{5,1},{6,2},{7,3},{8,12},{9,13},{10,... | collective-permute-start | bytes 3080 | tf_op jit(solution)/shard_map/ppermute | solution.py:32
  305.9 3.1 collective-permute-done.15
  309.2 9.3 %collective-permute-start.16 = (f32[2,128]{1,0:T(2,128)S(1)}, f32[2,128]{1,0:T(2,128)S(1)}, u32[]{:S(2)}, u32[]{:S(2)}) collective-permute-start(f32[2,128]{1,0:T(2,128)S(1)} %fusion.66), channel_id=1, source_target_pairs={{0,8},{1,9},{2,10},{3,11},{4,12},{5,13},{6,14},{7,15},{8,0},{9,1},... | collective-permute-start | bytes 3080 | tf_op jit(solution)/shard_map/ppermute | solution.py:32
  318.5 3.7 collective-permute-done.16
  322.8 7.2 %collective-permute-start.17 = (f32[2,128]{1,0:T(2,128)S(1)}, f32[2,128]{1,0:T(2,128)S(1)}, u32[]{:S(2)}, u32[]{:S(2)}) collective-permute-start(f32[2,128]{1,0:T(2,128)S(1)} %fusion.58), channel_id=1, source_target_pairs={{0,16},{1,17},{2,18},{3,19},{4,20},{5,21},{6,22},{7,23},{8,24},{9,... | collective-permute-start | bytes 3080 | tf_op jit(solution)/shard_map/ppermute | solution.py:32
  331.4 1.9 collective-permute-start.18
  333.3 2.4 collective-permute-done.18
  336.2 2.7 collective-permute-start.19
  338.9 3.1 collective-permute-done.19
  342.6 1.9 collective-permute-start.20
  344.8 2.2 collective-permute-done.20
  347.8 3.0 collective-permute-start.21
  350.8 1.7 convolution_bitcast_fusion
  359.8 1.1 multiply_reduce_fusion
  360.9 103.7 %psum.31 = f32[2]{0:T(128)S(1)} all-reduce(f32[2]{0:T(128)S(1)} %get-tuple-element.19), channel_id=1, replica_groups=mesh['gx'=32,'gy'=16] {'gx','gy'}, use_global_device_ids=true, to_apply=%region_6.0 | all-reduce | flops 2 | bytes 16 | tf_op jit(solution)/shard_map/psum | solution.py:127
  (128 shorter events, 25.0 us)
Async XLA Ops:
  0.6 1.2 copy-start
  0.6 2.5 copy-start.4
  0.7 8.0 %copy-start.1 = (f32[1,1,8,128,128]{4,3,2,1,0:T(8,128)S(1)}, f32[1,1,8,128,128]{4,3,2,1,0:T(8,128)}, u32[]{:S(2)}) copy-start(f32[1,1,8,128,128]{4,3,2,1,0:T(8,128)} %param.13) | copy-start | bytes 1572868
  0.7 65.9 %copy-start.2 = (f32[4,4,128,128]{3,2,1,0:T(8,128)S(1)}, f32[4,4,128,128]{3,2,1,0:T(8,128)}, u32[]{:S(2)}) copy-start(f32[4,4,128,128]{3,2,1,0:T(8,128)} %param.10) | copy-start | bytes 3145732
  3.4 5.3 %collective-permute-start = (f32[2,128]{1,0:T(2,128)S(1)}, f32[2,128]{1,0:T(2,128)S(1)}, u32[]{:S(2)}, u32[]{:S(2)}) collective-permute-start(f32[2,128]{1,0:T(2,128)S(1)} %fusion.94), channel_id=1, source_target_pairs={{0,1},{1,0},{2,3},{3,2},{4,5},{5,4},{6,7},{7,6},{8,9},{9,8},{10,11... | collective-permute-start | bytes 3080 | tf_op jit(solution)/shard_map/ppermute | solution.py:32
  8.8 5.9 %collective-permute-start.1 = (f32[2,128]{1,0:T(2,128)S(1)}, f32[2,128]{1,0:T(2,128)S(1)}, u32[]{:S(2)}, u32[]{:S(2)}) collective-permute-start(f32[2,128]{1,0:T(2,128)S(1)} %fusion.86), channel_id=1, source_target_pairs={{0,2},{1,3},{2,0},{3,1},{4,6},{5,7},{6,4},{7,5},{8,10},{9,11},{10,... | collective-permute-start | bytes 3080 | tf_op jit(solution)/shard_map/ppermute | solution.py:32
  14.9 9.8 %collective-permute-start.2 = (f32[2,128]{1,0:T(2,128)S(1)}, f32[2,128]{1,0:T(2,128)S(1)}, u32[]{:S(2)}, u32[]{:S(2)}) collective-permute-start(f32[2,128]{1,0:T(2,128)S(1)} %fusion.78), channel_id=1, source_target_pairs={{0,4},{1,5},{2,6},{3,7},{4,0},{5,1},{6,2},{7,3},{8,12},{9,13},{10,... | collective-permute-start | bytes 3080 | tf_op jit(solution)/shard_map/ppermute | solution.py:32
  24.8 14.0 %collective-permute-start.3 = (f32[2,128]{1,0:T(2,128)S(1)}, f32[2,128]{1,0:T(2,128)S(1)}, u32[]{:S(2)}, u32[]{:S(2)}) collective-permute-start(f32[2,128]{1,0:T(2,128)S(1)} %fusion.70), channel_id=1, source_target_pairs={{0,8},{1,9},{2,10},{3,11},{4,12},{5,13},{6,14},{7,15},{8,0},{9,1},... | collective-permute-start | bytes 3080 | tf_op jit(solution)/shard_map/ppermute | solution.py:32
  39.0 10.0 %collective-permute-start.4 = (f32[2,128]{1,0:T(2,128)S(1)}, f32[2,128]{1,0:T(2,128)S(1)}, u32[]{:S(2)}, u32[]{:S(2)}) collective-permute-start(f32[2,128]{1,0:T(2,128)S(1)} %fusion.62), channel_id=1, source_target_pairs={{0,16},{1,17},{2,18},{3,19},{4,20},{5,21},{6,22},{7,23},{8,24},{9,... | collective-permute-start | bytes 3080 | tf_op jit(solution)/shard_map/ppermute | solution.py:32
  49.1 4.3 collective-permute-start.5
  53.6 5.8 %collective-permute-start.6 = (f32[2,128]{1,0:T(2,128)S(1)}, f32[2,128]{1,0:T(2,128)S(1)}, u32[]{:S(2)}, u32[]{:S(2)}) collective-permute-start(f32[2,128]{1,0:T(2,128)S(1)} %fusion.46), channel_id=1, source_target_pairs={{0,64},{1,65},{2,66},{3,67},{4,68},{5,69},{6,70},{7,71},{8,72},{9,... | collective-permute-start | bytes 3080 | tf_op jit(solution)/shard_map/ppermute | solution.py:32
  59.6 4.3 collective-permute-start.7
  64.1 6.0 %copy-start.3 = (f32[1,1,9,128,128]{4,3,2,1,0:T(8,128)S(1)}, f32[1,1,9,128,128]{4,3,2,1,0:T(8,128)}, u32[]{:S(2)}) copy-start(f32[1,1,9,128,128]{4,3,2,1,0:T(8,128)} %param.15) | copy-start | bytes 1769476
  64.1 6.0 %collective-permute-start.8 = (f32[2,128]{1,0:T(2,128)S(1)}, f32[2,128]{1,0:T(2,128)S(1)}, u32[]{:S(2)}, u32[]{:S(2)}) collective-permute-start(f32[2,128]{1,0:T(2,128)S(1)} %fusion.30), channel_id=1, source_target_pairs={{0,256},{1,257},{2,258},{3,259},{4,260},{5,261},{6,262},{7,263},{8... | collective-permute-start | bytes 3080 | tf_op jit(solution)/shard_map/ppermute | solution.py:32
  73.1 0.9 copy-start.6
  74.2 1.0 copy-start.7
  75.2 8.8 %collective-permute-start.10 = (f32[3,1,128]{2,0,1:T(4,128)S(1)}, f32[3,1,128]{2,0,1:T(4,128)S(1)}, u32[]{:S(2)}, u32[]{:S(2)}) collective-permute-start(f32[3,1,128]{2,0,1:T(4,128)S(1)} %get-tuple-element.16), channel_id=1, source_target_pairs={{16,0},{32,16},{48,32},{64,48},{80,64},{96,80},{112,96},{128,112},... | collective-permute-start | bytes 4616 | tf_op jit(solution)/shard_map/ppermute | solution.py:22
  82.0 3.1 collective-permute-start.9
  85.2 3.0 collective-permute-start.11
  86.8 4.7 %collective-permute-start.12 = (f32[3,18,1]{2,0,1:T(4,128)S(1)}, f32[3,18,1]{2,0,1:T(4,128)S(1)}, u32[]{:S(2)}, u32[]{:S(2)}) collective-permute-start(f32[3,18,1]{2,0,1:T(4,128)S(1)} %get-tuple-element.9), channel_id=1, source_target_pairs={{1,0},{2,1},{3,2},{4,3},{5,4},{6,5},{7,6},{8,7},{9,8},{10,9},{11,1... | collective-permute-start | bytes 656 | tf_op jit(solution)/shard_map/ppermute | solution.py:22
  91.7 0.7 copy-start.5
  190.4 98.8 %copy-start.18 = (f32[2]{0:T(128)}, f32[2]{0:T(128)S(1)}, u32[]{:S(2)}) copy-start(f32[2]{0:T(128)S(1)} %psum.29) | copy-start | bytes 28
  289.2 0.6 copy-start.16
  290.6 4.6 collective-permute-start.13
  295.4 5.2 %collective-permute-start.14 = (f32[2,128]{1,0:T(2,128)S(1)}, f32[2,128]{1,0:T(2,128)S(1)}, u32[]{:S(2)}, u32[]{:S(2)}) collective-permute-start(f32[2,128]{1,0:T(2,128)S(1)} %fusion.82), channel_id=1, source_target_pairs={{0,2},{1,3},{2,0},{3,1},{4,6},{5,7},{6,4},{7,5},{8,10},{9,11},{10,... | collective-permute-start | bytes 3080 | tf_op jit(solution)/shard_map/ppermute | solution.py:32
  300.8 8.2 %collective-permute-start.15 = (f32[2,128]{1,0:T(2,128)S(1)}, f32[2,128]{1,0:T(2,128)S(1)}, u32[]{:S(2)}, u32[]{:S(2)}) collective-permute-start(f32[2,128]{1,0:T(2,128)S(1)} %fusion.74), channel_id=1, source_target_pairs={{0,4},{1,5},{2,6},{3,7},{4,0},{5,1},{6,2},{7,3},{8,12},{9,13},{10,... | collective-permute-start | bytes 3080 | tf_op jit(solution)/shard_map/ppermute | solution.py:32
  309.2 13.0 %collective-permute-start.16 = (f32[2,128]{1,0:T(2,128)S(1)}, f32[2,128]{1,0:T(2,128)S(1)}, u32[]{:S(2)}, u32[]{:S(2)}) collective-permute-start(f32[2,128]{1,0:T(2,128)S(1)} %fusion.66), channel_id=1, source_target_pairs={{0,8},{1,9},{2,10},{3,11},{4,12},{5,13},{6,14},{7,15},{8,0},{9,1},... | collective-permute-start | bytes 3080 | tf_op jit(solution)/shard_map/ppermute | solution.py:32
  322.2 0.6 copy-start.8
  322.8 8.0 %collective-permute-start.17 = (f32[2,128]{1,0:T(2,128)S(1)}, f32[2,128]{1,0:T(2,128)S(1)}, u32[]{:S(2)}, u32[]{:S(2)}) collective-permute-start(f32[2,128]{1,0:T(2,128)S(1)} %fusion.58), channel_id=1, source_target_pairs={{0,16},{1,17},{2,18},{3,19},{4,20},{5,21},{6,22},{7,23},{8,24},{9,... | collective-permute-start | bytes 3080 | tf_op jit(solution)/shard_map/ppermute | solution.py:32
  330.8 0.6 copy-start.10
  331.4 4.3 collective-permute-start.18
  335.7 0.6 copy-start.12
  336.2 5.8 %collective-permute-start.19 = (f32[2,128]{1,0:T(2,128)S(1)}, f32[2,128]{1,0:T(2,128)S(1)}, u32[]{:S(2)}, u32[]{:S(2)}) collective-permute-start(f32[2,128]{1,0:T(2,128)S(1)} %fusion.42), channel_id=1, source_target_pairs={{0,64},{1,65},{2,66},{3,67},{4,68},{5,69},{6,70},{7,71},{8,72},{9,... | collective-permute-start | bytes 3080 | tf_op jit(solution)/shard_map/ppermute | solution.py:32
  342.0 0.6 copy-start.14
  342.6 4.4 collective-permute-start.20
  347.8 5.8 %collective-permute-start.21 = (f32[2,128]{1,0:T(2,128)S(1)}, f32[2,128]{1,0:T(2,128)S(1)}, u32[]{:S(2)}, u32[]{:S(2)}) collective-permute-start(f32[2,128]{1,0:T(2,128)S(1)} %fusion.26), channel_id=1, source_target_pairs={{0,256},{1,257},{2,258},{3,259},{4,260},{5,261},{6,262},{7,263},{8... | collective-permute-start | bytes 3080 | tf_op jit(solution)/shard_map/ppermute | solution.py:32
  354.8 0.7 copy-start.15
  355.7 0.7 copy-start.13
  356.5 0.7 copy-start.11
  357.4 0.7 copy-start.9
  360.9 103.8 %copy-start.19 = (f32[2]{0:T(128)S(1)}, f32[2]{0:T(128)}, u32[]{:S(2)}) copy-start(f32[2]{0:T(128)} %copy-done.18) | copy-start | bytes 28
  464.7 0.7 copy-start.17
